TPU v7x, 32 devices: a whole 2x2x4 slice. The times are simulated.
32 devices in a mesh: seq: 8 (over y, x, core), tensor: 4 (over z).
Axes of the slice: x: 2, y: 2, z: 4, core: 2. Of those that a mesh axis runs over, the one named last changes fastest.
Arguments:
- inputs: bfloat16 [1, 1024, 4096], P(None, 'seq', 'tensor'), may hold values from -6 to 6
- projections: bfloat16 [1, 1024, 1024], P(None, 'seq', 'tensor'), may hold values from -4 to 4
- step_raw: float32 [64, 1, 1024], P('tensor', None, 'seq'), may hold values from -16 to 1.2, as said below
- rate_log: float32 [64], P('tensor'), may hold values from -0.7 to 0.7
- out_grad: bfloat16 [1, 1024, 4096], P(None, 'seq', 'tensor'), may hold values from -24 to 24
Outputs:
- grad_inputs: bfloat16 [1, 1024, 4096], P(None, 'seq', 'tensor')
- grad_projections: bfloat16 [1, 1024, 1024], P(None, 'seq', 'tensor')
- grad_step_raw: float32 [64, 1, 1024], P('tensor', None, 'seq')
- grad_rate_log: float32 [64], P('tensor')
Inputs may be any that keep to these rules, and one draw needn't show every extreme that they name: `step_raw`: log(exp(step) - 1) of a positive step size.
All inputs are finite; a program needn't handle non-finite values.
Results may differ from a plain program's by a relative error of at most 0.001.
Values may be sent and summed in bfloat16 or wider, within the bound.
A program may use at most 192 MiB of HBM per device.

v0:
```python
import jax
import jax.numpy as jnp
from jax import lax
from jax.sharding import PartitionSpec as P

SPAN = 128


HIGHEST = lax.Precision.HIGHEST


def entering_2(value, axis, combine, identity, reverse):
    count, index = (lax.axis_size(axis), lax.axis_index(axis))
    everything = jax.tree.map(lambda part: lax.all_gather(part, axis), value)
    start = jax.tree.map(
        lambda part, zero: jnp.broadcast_to(jnp.asarray(zero, part.dtype), part.shape),
        value,
        identity,
    )

    def step(k, before):
        at = count - 1 - k if reverse else k
        reached = at > index if reverse else at < index
        new = combine(before, jax.tree.map(lambda part: part[at], everything))
        return jax.tree.map(lambda a, b: jnp.where(reached, a, b), new, before)

    return lax.fori_loop(0, count, step, start)


def swapped(value, axis, apart):
    mask = 2**apart
    pairs = [(source, source ^ mask) for source in range(lax.axis_size(axis))]
    return lax.ppermute(value, axis, pairs)


def segment_forward(scaled, inject, readout, log_decay, entering):
    seq_count, tok_count, head_count, head_width = scaled.shape
    state_width = inject.shape[-1]
    blocks = tok_count // SPAN
    scaled_blocks = scaled.reshape(seq_count, blocks, SPAN, head_count, head_width).transpose(
        1, 0, 2, 3, 4
    )
    inject_blocks = inject.reshape(seq_count, blocks, SPAN, state_width).transpose(1, 0, 2, 3)
    readout_blocks = readout.reshape(seq_count, blocks, SPAN, state_width).transpose(1, 0, 2, 3)
    decay_blocks = log_decay.reshape(seq_count, head_count, blocks, SPAN).transpose(2, 0, 1, 3)
    position = jnp.arange(SPAN)
    causal = position[:, None] >= position[None, :]

    def advance(running, pieces):
        scaled_piece, inject_piece, readout_piece, decay_piece = pieces
        cumulative = jnp.cumsum(decay_piece, axis=-1)
        scores = jnp.einsum("sin,sjn->sij", readout_piece, inject_piece, precision=HIGHEST)
        log_gap = jnp.where(causal, cumulative[..., :, None] - cumulative[..., None, :], 0.0)
        weight = jnp.where(causal, jnp.exp(log_gap), 0.0) * scores[:, None]
        within = jnp.einsum("shij,sjhp->sihp", weight, scaled_piece, precision=HIGHEST)
        carried = jnp.einsum("sin,shpn->sihp", readout_piece, running, precision=HIGHEST)
        carried = carried * jnp.exp(cumulative).transpose(0, 2, 1)[..., None]
        to_end = jnp.exp(cumulative[..., -1:] - cumulative)
        updated = jnp.exp(cumulative[..., -1])[..., None, None] * running
        updated = updated + jnp.einsum(
            "shj,sjhp,sjn->shpn", to_end, scaled_piece, inject_piece, precision=HIGHEST
        )
        return (updated, within + carried)

    closing, outputs = lax.scan(
        advance, entering, (scaled_blocks, inject_blocks, readout_blocks, decay_blocks)
    )
    outputs = outputs.transpose(1, 0, 2, 3, 4).reshape(seq_count, tok_count, head_count, head_width)
    return (outputs, closing)


def prepare(values, step_raw, rate_log):
    step_width = jax.nn.softplus(step_raw)
    log_decay = step_width.transpose(1, 0, 2) * (-jnp.exp(rate_log))[None, :, None]
    scaled = values * step_width.transpose(1, 2, 0)[..., None]
    return (scaled, log_decay)


def carry_chain(decay, summaries, backward):

    def combine(earlier, later):
        return (earlier[0] * later[0], later[0][..., None, None] * earlier[1] + later[1])

    identity = (jnp.ones_like(decay), jnp.zeros_like(summaries))
    return entering_2((decay, summaries), "seq", combine, identity, backward)[1]


def per_device(inputs, projections, step_raw, rate_log, out_grad):
    seq_count, tok_count, feature_count = inputs.shape
    head_count = step_raw.shape[0]
    head_width = feature_count // head_count
    state_width = projections.shape[2]
    partner = swapped(projections, "tensor", 0)
    is_even = lax.axis_index("tensor") % 2 == 0
    inject = jnp.where(is_even, projections, partner).astype(jnp.float32)
    readout = jnp.where(is_even, partner, projections).astype(jnp.float32)
    values = inputs.astype(jnp.float32).reshape(seq_count, tok_count, head_count, head_width)
    cotangent = out_grad.astype(jnp.float32).reshape(seq_count, tok_count, head_count, head_width)
    scaled, log_decay = prepare(values, step_raw, rate_log)
    decay = jnp.exp(jnp.sum(log_decay, axis=-1))
    empty_state = jnp.zeros((seq_count, head_count, head_width, state_width), jnp.float32)
    summary = segment_forward(scaled, inject, readout, log_decay, empty_state)[1]
    state_in = carry_chain(decay, summary, False)

    def outputs_of_state(entering):
        return segment_forward(scaled, inject, readout, log_decay, entering)[0]

    _, pull_state = jax.vjp(outputs_of_state, empty_state)
    own_term = pull_state(cotangent)[0]
    state_later = carry_chain(decay, own_term, True)

    def local_pass(values, inject, readout, steps_here, rates_here):
        scaled_here, decay_here = prepare(values, steps_here, rates_here)
        return segment_forward(scaled_here, inject, readout, decay_here, state_in)

    _, pull = jax.vjp(local_pass, values, inject, readout, step_raw, rate_log)
    grad_values, grad_inject, grad_readout, grad_steps, grad_rates = pull((cotangent, state_later))
    keeping = jnp.where(is_even, grad_inject, grad_readout)
    sending = jnp.where(is_even, grad_readout, grad_inject)
    grad_pair = (keeping + swapped(sending, "tensor", 0)).astype(jnp.bfloat16)
    grad_rate = lax.psum(grad_rates, "seq")
    grad_inputs = grad_values.reshape(seq_count, tok_count, feature_count).astype(jnp.bfloat16)
    return (grad_inputs, grad_pair, grad_steps, grad_rate)


def solution(mesh):
    in_specs = (
        P(None, "seq", "tensor"),
        P(None, "seq", "tensor"),
        P("tensor", None, "seq"),
        P("tensor"),
        P(None, "seq", "tensor"),
    )
    out_specs = (
        P(None, "seq", "tensor"),
        P(None, "seq", "tensor"),
        P("tensor", None, "seq"),
        P("tensor"),
    )
    return jax.shard_map(
        per_device, mesh=mesh, in_specs=in_specs, out_specs=out_specs, check_vma=False
    )
```

profile of v0, /device:TPU:0, one launch (start us, length us, event | category | flops | bytes accessed | tf_op | source)
XLA Modules:
  0.0 182.8 jit_solution(13999067286679097011)
XLA Ops:
  7.2 0.9 copy.84
  8.2 3.1 %collective-permute-start = (bf16[1,128,256]{1,2,0:T(8,128)(2,1)S(1)}, bf16[1,128,256]{1,2,0:T(8,128)(2,1)S(1)}, u32[]{:S(2)}, u32[]{:S(2)}) collective-permute-start(bf16[1,128,256]{1,2,0:T(8,128)(2,1)S(1)} %copy.84), channel_id=1, source_target_pairs={{0,1},{1,0},{2,3},{3,2},{4,5},{5,4},{6,7},{7,6},{8,9},{9,8},{10,11... | collective-permute-start | bytes 196616 | tf_op jit(solution)/shard_map/ppermute | solution.py:33
  11.9 1.4 fusion.51
  13.8 1.1 copy.83
  15.0 1.6 convolution_add_fusion.1
  16.7 1.1 copy.96
  17.8 0.7 fusion.49
  19.2 1.6 convolution_add_fusion
  20.9 1.2 dynamic-slice.4
  23.3 1.3 exponential_dynamic-update-slice_fusion
  24.6 14.4 %all-reduce.2 = f32[128]{0:T(128)} all-reduce(f32[128]{0:T(128)} %exponential_dynamic-update-slice_fusion), channel_id=2, replica_groups=mesh['seq'=8,'tensor'=4] {'seq'}, use_global_device_ids=true, to_apply=%add.2 | all-reduce | flops 128 | bytes 1024
  39.0 1.3 reshape.806
  40.3 0.9 mul.365
  41.2 2.0 %copy.95 = f32[1,128,1024]{2,1,0:T(8,128)} copy(f32[1,128,1024]{1,2,0:T(8,128)} %bitcast.198) | data formatting | bytes 1048576 | tf_op jit(solution)/shard_map/mul | solution.py:75
  44.1 2.2 %fusion.13 = (f32[16,128]{1,0:T(8,128)}, f32[16,128]{1,0:T(8,128)}, f32[128,128]{0,1:T(8,128)}) fusion(f32[128,128]{0,1:T(8,128)S(1)} %fusion.35, f32[16,128]{1,0:T(8,128)S(1)} %bitcast.200, pred[128,128]{0,1:T(8,128)(4,1)S(1)} %iota_compare_fusion, bf16[16,64,128]{2,1,0:T(8,128)(2,1)S(1)} %bitcast.195, f32[128,16,64]{0,2,1:T(8,128)S(1)} %bitcast.187, ...), kind=kOutput, calls=%fused_computation.30 | convolution fusion | flops 204320768 | bytes 966656 | tf_op jit(solution)/shard_map/transpose(jvp())/while/body/eval_jaxpr/shij,sjhp->sihp/dot_general | solution.py:55
  46.3 25.3 %all-gather.6.cloned.1.call-done = f32[128,64,256]{2,1,0:T(8,128)} async-done(((f32[16,64,256]{2,1,0:T(8,128)}), f32[128,64,256]{2,1,0:T(8,128)}) %all-gather.6.cloned.1.call-update) | async-done | bytes 8388624 | tf_op jit(solution)/shard_map/all_gather | solution.py:14
  71.6 21.2 %while.24 = (s32[]{:T(128)}, f32[1,16,64,256]{3,2,1,0:T(8,128)S(1)}, s32[]{:T(128)}, f32[8,1,16]{2,1,0:T(1,128)}, f32[8,1,16,64,256]{4,3,2,1,0:T(8,128)}, /*index=5*/s32[]{:T(128)}, s32[]{:T(128)}, s32[]{:T(128)}, s32[]{:T(128)}) while((s32[]{:T(128)}, f32[1,16,64,256]{3,2,1,0:T(8,128)S(1)}, s32[]{:T(128)}, f32[8,1,16]{2,1,0:T(1,128)}, ...), condition=%wide.region_3.4_spmd.clone, body=%wide.region_2.3_spmd.clone.sunk | while | flops 1048584 | bytes 3146095 | solution.py:27
  71.6 1.2 dynamic-slice_bitcast_fusion.4
  72.8 1.5 fusion.60
  74.2 1.2 dynamic-slice_bitcast_fusion.4
  75.4 1.5 fusion.60
  76.9 1.1 dynamic-slice_bitcast_fusion.4
  78.0 1.5 fusion.60
  79.5 1.2 dynamic-slice_bitcast_fusion.4
  80.7 1.6 fusion.60
  82.3 1.1 dynamic-slice_bitcast_fusion.4
  83.4 1.5 fusion.60
  84.9 1.2 dynamic-slice_bitcast_fusion.4
  86.1 1.5 fusion.60
  87.6 1.2 dynamic-slice_bitcast_fusion.4
  88.7 1.5 fusion.60
  90.2 1.1 dynamic-slice_bitcast_fusion.4
  91.3 1.5 fusion.60
  92.8 3.2 %convolution_bitcast_fusion.5 = f32[1,128,256]{1,2,0:T(8,128)} fusion(f32[1,16,64,256]{3,2,1,0:T(8,128)S(1)} %get-tuple-element.553, f32[128,16,64]{0,2,1:T(8,128)S(1)} %bitcast.188, f32[128,16]{0,1:T(8,128)S(1)} %fusion.49, f32[128,16]{0,1:T(8,128)} %copy-done.2), kind=kOutput, calls=%fused_computation.17 | convolution fusion | flops 402915328 | bytes 1720320 | tf_op jit(solution)/shard_map/transpose(jvp())/while/body/eval_jaxpr/shj,sjhp,sjn->shpn/dot_general | solution.py:60
  95.9 2.1 %multiply_reduce_fusion.2 = (f32[128,16]{0,1:T(8,128)}, f32[128,16,64]{0,2,1:T(8,128)}) fusion(f32[128,16,64]{0,2,1:T(8,128)S(1)} %bitcast.189, f32[128,16]{0,1:T(8,128)S(1)} %fusion.49, bf16[1,128,256]{1,2,0:T(8,128)(2,1)S(1)} %get-tuple-element.658, f32[1,16,64,256]{3,2,1,0:T(8,128)S(1)} %get-tuple-element.553), kind=kOutput, calls=%fused_computation.33 | convolution fusion | flops 403044352 | bytes 2179072 | tf_op jit(solution)/shard_map/transpose(jvp())/while/body/eval_jaxpr/shj,sjhp,sjn->shpn/dot_general | solution.py:60
  98.0 29.9 %all-gather.8.cloned.1.call-done = f32[128,64,256]{2,1,0:T(8,128)} async-done(((f32[16,64,256]{2,1,0:T(8,128)}), f32[128,64,256]{2,1,0:T(8,128)}) %all-gather.8.cloned.1.call-update) | async-done | bytes 8388624 | tf_op jit(solution)/shard_map/all_gather | solution.py:14
  127.9 16.9 %while.25 = (s32[]{:T(128)}, f32[1,16,64,256]{3,2,1,0:T(8,128)S(1)}, s32[]{:T(128)}, f32[8,1,16]{2,1,0:T(1,128)}, f32[8,1,16,64,256]{4,3,2,1,0:T(8,128)}, /*index=5*/s32[]{:T(128)}, s32[]{:T(128)}) while((s32[]{:T(128)}, f32[1,16,64,256]{3,2,1,0:T(8,128)S(1)}, s32[]{:T(128)}, f32[8,1,16]{2,1,0:T(1,128)}, ...), condition=%wide.region_6.7_spmd.clone, body=%wide.region_5.6_spmd.clone.sunk | while | flops 1048580 | bytes 3146033 | solution.py:27
  128.4 1.5 fusion.61
  129.9 0.7 dynamic-slice_bitcast_fusion.5
  130.6 1.5 fusion.61
  132.7 1.5 fusion.61
  134.8 1.5 fusion.61
  136.3 0.7 dynamic-slice_bitcast_fusion.5
  137.0 1.5 fusion.61
  139.0 1.5 fusion.61
  140.5 0.7 dynamic-slice_bitcast_fusion.5
  141.2 1.5 fusion.61
  142.7 0.7 dynamic-slice_bitcast_fusion.5
  143.4 1.5 fusion.61
  144.8 2.4 %convolution_bitcast_fusion.4 = f32[128,256]{0,1:T(8,128)} fusion(f32[128,16,64]{0,2,1:T(8,128)S(1)} %bitcast.192, f32[1,16,64,256]{3,2,1,0:T(8,128)S(1)} %get-tuple-element.554), kind=kOutput, calls=%fused_computation.16 | convolution fusion | flops 402653184 | bytes 1703936 | tf_op jit(solution)/shard_map/transpose(jvp())/while/body/eval_jaxpr/sin,shpn->sihp/dot_general | solution.py:56
  147.3 0.7 multiply_reduce_fusion
  148.0 2.4 %multiply_reduce_fusion.3 = (f32[128,16]{0,1:T(8,128)S(1)}, f32[1,128,16,64]{1,3,2,0:T(8,128)S(1)}) fusion(f32[1,128,16,64]{1,3,2,0:T(8,128)S(1)} %bitcast.190, bf16[16,64,128]{2,1,0:T(8,128)(2,1)S(1)} %bitcast.196, f32[128,128]{0,1:T(8,128)} %copy-done.3, f32[16,128]{1,0:T(8,128)S(1)} %bitcast.201, pred[128,128]{0,1:T(8,128)(4,1)} %copy-done.4, ...), kind=kOutput, calls=%fused_computation.34 | convolution fusion | flops 202897408 | bytes 1941504 | tf_op jit(solution)/shard_map/transpose(jvp())/while/body/eval_jaxpr/shij,sjhp->sihp/dot_general | solution.py:55
  151.3 0.9 fusion.48
  152.2 0.7 copy.104
  153.1 0.8 fusion.46
  153.9 1.2 reduce_window_sum.41
  155.3 0.7 negate_multiply_fusion
  155.9 1.2 fusion.4
  157.1 1.2 broadcast_select_fusion
  158.3 1.6 collective-permute-start.1
  159.8 13.3 %psum.7 = f32[16]{0:T(128)} all-reduce(f32[16]{0:T(128)S(1)} %negate_multiply_fusion), channel_id=1, replica_groups=mesh['seq'=8,'tensor'=4] {'seq'}, use_global_device_ids=true, to_apply=%region_15.16 | all-reduce | flops 16 | bytes 128 | tf_op jit(solution)/shard_map/psum | solution.py:121
  173.1 0.8 multiply_convert_fusion
  173.9 1.3 fusion.42
  175.2 0.7 copy.109
  (43 shorter events, 7.0 us)
Async XLA Ops:
  7.2 64.4 %all-gather.6.cloned.1.call-start = ((), (), s32[]{:S(2)}) async-start(), calls=%async_computation | async-start | bytes 9437184 | tf_op jit(solution)/shard_map/all_gather | solution.py:14
  8.2 6.8 %collective-permute-start = (bf16[1,128,256]{1,2,0:T(8,128)(2,1)S(1)}, bf16[1,128,256]{1,2,0:T(8,128)(2,1)S(1)}, u32[]{:S(2)}, u32[]{:S(2)}) collective-permute-start(bf16[1,128,256]{1,2,0:T(8,128)(2,1)S(1)} %copy.84), channel_id=1, source_target_pairs={{0,1},{1,0},{2,3},{3,2},{4,5},{5,4},{6,7},{7,6},{8,9},{9,8},{10,11... | collective-permute-start | bytes 196616 | tf_op jit(solution)/shard_map/ppermute | solution.py:33
  11.9 4.7 %copy-start.6 = (f32[16]{0:T(128)}, f32[16]{0:T(128)S(1)}, u32[]{:S(2)}) copy-start(f32[16]{0:T(128)S(1)} %exponential_negate_fusion) | copy-start | bytes 196
  13.8 7.1 %copy-start.5 = (f32[16]{0:T(128)}, f32[16]{0:T(128)S(1)}, u32[]{:S(2)}) copy-start(f32[16]{0:T(128)S(1)} %slice_reduce_fusion) | copy-start | bytes 196
  16.7 111.2 %all-gather.8.cloned.1.call-start = ((), (), s32[]{:S(2)}) async-start(), calls=%async_computation.1 | async-start | bytes 9437184 | tf_op jit(solution)/shard_map/all_gather | solution.py:14
  18.6 0.6 copy-start.2
  43.2 0.6 copy-start.4
  43.4 0.6 copy-start.3
  144.8 10.3 %copy-start.1 = (f32[16,1,128]{2,1,0:T(1,128)S(1)}, f32[16,1,128]{2,1,0:T(1,128)}, u32[]{:S(2)}) copy-start(f32[16,1,128]{2,1,0:T(1,128)} %param.11) | copy-start | bytes 24580
  147.3 25.9 %copy-start = (f32[1,128,1024]{2,1,0:T(8,128)S(1)}, f32[1,128,1024]{2,1,0:T(8,128)}, u32[]{:S(2)}) copy-start(f32[1,128,1024]{2,1,0:T(8,128)} %copy.95) | copy-start | bytes 1572868
  158.3 16.9 %collective-permute-start.1 = (f32[1,128,256]{1,2,0:T(8,128)S(1)}, f32[1,128,256]{1,2,0:T(8,128)S(1)}, u32[]{:S(2)}, u32[]{:S(2)}) collective-permute-start(f32[1,128,256]{1,2,0:T(8,128)S(1)} %get-tuple-element.660), channel_id=1, source_target_pairs={{0,1},{1,0},{2,3},{3,2},{4,5},{5,4},{6,7},{7,6},{8,9},{9,8},{10,11... | collective-permute-start | bytes 393224 | tf_op jit(solution)/shard_map/ppermute | solution.py:33
Sparse Core Ops, SparseCore 0:
  16.8 54.7 all-gather.5
  73.4 54.3 all-gather.7
where the time goes:
time: 184 us; the launch traced here: 183 us
  waiting for transfers between devices  55.2 us (30%)
  other arithmetic  33.3 us (18%)
  local copies, waits for them, and re-layouts  28 us (15%)
  blocking collectives  27.7 us (15%)
  matrix products  18.7 us (10%)
  between operations  14.9 us (8%)
  starting transfers between devices  4.72 us (3%)
    all_gather x2, waiting for transfers between devices, entering_2(): everything = jax.tree.map(lambda part: lax.all_gather(part, axis), value)  55.2 us
    select_n x16, other arithmetic, step(): return jax.tree.map(lambda a, b: jnp.where(reached, a, b), new, before)  23.4 us
    unnamed x1, blocking collectives  14.4 us
    mul x16, local copies, waits for them, and re-layouts, combine(): later[0][..., None, None] * earlier[1] + later[1]  14.4 us
    psum x1, blocking collectives, per_device(): grad_rate = lax.psum(grad_rates, 'seq')  13.3 us
    unnamed x20, local copies, waits for them, and re-layouts  7.08 us
    dot_general x3, matrix products, advance(): jnp.einsum('shj,sjhp,sjn->shpn', to_end, scaled_piece, inject_piece, prec...  6.85 us
    dot_general x3, matrix products, advance(): jnp.einsum('sin,shpn->sihp', readout_piece, running, precision=HIGHEST)  4.64 us
  transfers between devices with their start and end apart: 4, of which 2 were waited for; matrix products, arithmetic and copies ran while one was open for 25% of the time, Pallas kernels for 0%

commit v1 on v0

v1 whole, which is shorter than its diff:
```python
import functools

import jax
import jax.numpy as jnp
from jax import lax
from jax.experimental import pallas as pl
from jax.experimental.pallas import tpu as pltpu
from jax.sharding import PartitionSpec as P

MESH = pl.DeviceIdType.MESH
HIGHEST = lax.Precision.HIGHEST
F32, BF16 = jnp.float32, jnp.bfloat16
CHUNK = 256
NT = (((1,), (1,)), ((), ()))
TN = (((0,), (0,)), ((), ()))
NN = (((1,), (0,)), ((), ()))


def dot(a, b, dims=NN):
    return lax.dot_general(a, b, dims, preferred_element_type=F32)


def split(a):
    high = a.astype(BF16)
    return high, (a - high.astype(F32)).astype(BF16)


def kernel(seq_count, head_width, x_ref, proj_ref, raw_ref, rate_ref, g_ref,
           gx_ref, gp_ref, gs_ref, gr_ref,
           other, local, near, tots, totr, lasts, lastr, passed, wide, du_ref,
           pair_s, pair_r, rate_s, rate_r,
           s_other, s_near, s_far, s_tot, s_last, s_pass, s_pair, s_rate):
    span, width = x_ref.shape
    heads = raw_ref.shape[0]
    state = proj_ref.shape[1]
    chunks = width // CHUNK
    half = chunks // 2
    levels = seq_count.bit_length() - 1
    me = lax.axis_index("seq")
    core = lax.rem(me, 2)
    tensor = lax.axis_index("tensor")
    even = lax.rem(tensor, 2) == 0
    buddy = tensor + 1 - 2 * lax.rem(tensor, 2)

    def partner(bit):
        place = 2**bit
        upper = lax.rem(me // place, 2)
        return me + place - 2 * place * upper, upper

    barrier = pltpu.get_barrier_semaphore()
    for apart in range(1, seq_count):
        pl.semaphore_signal(barrier, inc=1, device_id={"seq": lax.rem(me + apart, seq_count)},
                            device_id_type=MESH)
    pl.semaphore_signal(barrier, inc=1, device_id={"tensor": buddy}, device_id_type=MESH)
    pl.semaphore_wait(barrier, seq_count)

    def send(src, dst, sems, at, **where):
        copy = pltpu.make_async_remote_copy(
            src_ref=src, dst_ref=dst, send_sem=sems.at[(0,) + at], recv_sem=sems.at[(1,) + at],
            device_id=where, device_id_type=MESH)
        copy.start()
        return copy

    swap = send(proj_ref, other, s_other, (), tensor=buddy)

    raw = raw_ref[...]
    small = jnp.exp(-jnp.abs(raw))
    one = 1.0 + small
    log1p = jnp.where(one == 1.0, small, jnp.log(one) * small / jnp.where(one == 1.0, 1.0, one - 1.0))
    step = jnp.maximum(raw, 0.0) + log1p
    sigmoid = jnp.where(raw >= 0, 1.0, small) / one
    rate = -jnp.exp(rate_ref[:, 0:1])
    log_decay = rate * step
    rows = lax.broadcasted_iota(jnp.int32, (span, span), 0)
    cols = lax.broadcasted_iota(jnp.int32, (span, span), 1)
    causal = cols >= rows
    cum = lax.dot_general(log_decay, causal.astype(F32), NN, precision=HIGHEST,
                          preferred_element_type=F32)
    total = cum[:, span - 1:span]
    at_row = lax.broadcasted_iota(jnp.int32, (heads, width), 0) * head_width
    at_col = lax.broadcasted_iota(jnp.int32, (heads, width), 1)
    spread = ((at_col >= at_row) & (at_col < at_row + head_width)).astype(F32).astype(BF16)
    spread3 = jnp.concatenate([spread, spread, spread], axis=0)

    def widen(a):
        high = a.astype(BF16)
        rest = a - high.astype(F32)
        mid = rest.astype(BF16)
        low = (rest - mid.astype(F32)).astype(BF16)
        return dot(jnp.concatenate([high, mid, low], axis=0), spread3, TN)

    def gather_heads(a):
        high = a.astype(BF16)
        rest = a - high.astype(F32)
        mid = rest.astype(BF16)
        return dot(spread, high, NT) + dot(spread, mid, NT)

    wide[0] = widen(step)
    wide[1] = widen(jnp.exp(total - cum))
    wide[2] = widen(jnp.exp(cum))
    swap.wait()
    own, theirs = proj_ref[...].astype(F32), other[...].astype(F32)
    b = jnp.where(even, own, theirs).astype(BF16)
    c = jnp.where(even, theirs, own).astype(BF16)

    for q in range(chunks):
        lanes = slice(q * CHUNK, (q + 1) * CHUNK)
        inj = x_ref[:, lanes].astype(F32) * wide[0, :, lanes] * wide[1, :, lanes]
        out = g_ref[:, lanes].astype(F32) * wide[2, :, lanes]
        high, low = split(inj)
        local[q, 0, :state] = dot(b, high, TN) + dot(b, low, TN)
        high, low = split(out)
        local[q, 1, :state] = dot(c, high, TN) + dot(c, low, TN)
        decay = jnp.broadcast_to(wide[2, span - 1:span, lanes], (8, CHUNK))
        local[q, 0, state:] = decay
        local[q, 1, state:] = decay

    mate, _ = partner(0)
    close = [send(local.at[(1 - core) * half + k], near.at[(1 - core) * half + k], s_near, (k,), seq=mate)
             for k in range(half)]
    rest = [send(local.at[core * half + k, core], near.at[core * half + k, core], s_far, (k,), seq=mate)
            for k in range(half)]

    is_up = core == 1

    def merge(up, f_own, r_own, d_own, f_in, r_in, d_in):
        f = jnp.where(up, 1.0, d_in) * f_own + jnp.where(up, d_own, 1.0) * f_in
        r = jnp.where(up, d_in, 1.0) * r_own + jnp.where(up, 1.0, d_own) * r_in
        return f, r, d_own * d_in

    sent = {}

    def put(level, k, f, r, d):
        target, upper = partner(level)
        d8 = jnp.broadcast_to(d, (8, CHUNK))
        if level == levels - 1:
            lasts[k, :state] = jnp.where(upper == 1, r, f)
            lasts[k, state:] = d8
            sent[level, k] = send(lasts.at[k], lastr.at[k], s_last, (k,), seq=target)
        else:
            tots[level - 1, k, 0, :state] = f
            tots[level - 1, k, 1, :state] = r
            tots[level - 1, k, 0, state:] = d8
            tots[level - 1, k, 1, state:] = d8
            sent[level, k] = send(tots.at[level - 1, k], totr.at[level - 1, k], s_tot,
                                  (level - 1, k), seq=target)

    for k in range(half):
        close[k].wait()
        q = core * half + k
        f, r, d = merge(is_up, local[q, 0, :state], local[q, 1, :state], local[q, 0, state:state + 1],
                        near[core * half + k, 0, :state], near[core * half + k, 1, :state],
                        near[core * half + k, 0, state:state + 1])
        put(1, k, f, r, d)

    scores = dot(b, c, NT)
    total_scores = jnp.zeros((span, span), F32)
    cum_t = jnp.transpose(cum)
    step_t = jnp.transpose(step)
    lane = lax.broadcasted_iota(jnp.int32, (span, 128), 1)
    per = 128 // head_width
    from_rows = []
    for p in range(width // 128):
        lanes = slice(p * 128, (p + 1) * 128)
        xs, gs = x_ref[:, lanes], g_ref[:, lanes]
        grown = jnp.zeros((span, 128), F32)
        for part in range(per):
            h = p * per + part
            mine = (lane >= part * head_width) & (lane < (part + 1) * head_width)
            inner = dot(jnp.where(mine, xs.astype(F32), 0.0).astype(BF16), gs, NT)
            gap = cum[h:h + 1, :] - cum_t[:, h:h + 1]
            fade = jnp.exp(jnp.where(causal, gap, -1e30))
            weight = fade * scores
            flow = inner * step_t[:, h:h + 1]
            total_scores = total_scores + flow * fade
            from_rows.append(jnp.sum(flow * weight, axis=0, keepdims=True))
            high, low = split(weight)
            grown = jnp.where(mine, dot(high, gs) + dot(low, gs), grown)
        du_ref[:, lanes] = grown
    row_part = jnp.concatenate(from_rows, axis=0)
    high, low = split(total_scores)
    grad_b = dot(high, c) + dot(low, c)
    grad_c = dot(high, b, TN) + dot(low, b, TN)

    zero = jnp.zeros((state, CHUNK), F32)
    ones = jnp.ones((1, CHUNK), F32)
    dp, dq = [ones] * half, [ones] * half
    for k in range(half):
        passed[core * half + k, 0] = zero
        passed[core * half + k, 1] = zero
    moved = []
    for level in range(1, levels):
        _, upper = partner(level)
        up = upper == 1
        for k in range(half):
            sent[level, k].wait()
            q = core * half + k
            if level == levels - 1:
                got = lastr[k, :state]
                before, after = passed[q, 0], passed[q, 1]
                passed[q, 0] = before + jnp.where(up, dp[k], 0.0) * got
                passed[q, 1] = after + jnp.where(up, 0.0, dq[k]) * got
                moved.append(send(passed.at[q], passed.at[q], s_pass, (k,), seq=mate))
            else:
                at = level - 1
                f_in, r_in = totr[at, k, 0, :state], totr[at, k, 1, :state]
                d_in = totr[at, k, 0, state:state + 1]
                passed[q, 0] = passed[q, 0] + jnp.where(up, dp[k], 0.0) * f_in
                passed[q, 1] = passed[q, 1] + jnp.where(up, 0.0, dq[k]) * r_in
                dp[k] = dp[k] * jnp.where(up, d_in, 1.0)
                dq[k] = dq[k] * jnp.where(up, 1.0, d_in)
                f, r, d = merge(up, tots[at, k, 0, :state], tots[at, k, 1, :state],
                                tots[at, k, 0, state:state + 1], f_in, r_in, d_in)
                put(level + 1, k, f, r, d)
    for copy in rest + moved:
        copy.wait()

    dcum = row_part
    last = []
    taken = []
    for q in range(chunks):
        lanes = slice(q * CHUNK, (q + 1) * CHUNK)
        before, after = passed[q, 0], passed[q, 1]
        side = near[q, 1 - core]
        joined = side[:state] + side[state:state + 1] * jnp.where(is_up, before, after)
        enter = jnp.where(is_up, joined, before)
        leave = jnp.where(is_up, after, joined)
        eh, el = split(enter)
        lh, ll = split(leave)
        xs, gs = x_ref[:, lanes].astype(F32), g_ref[:, lanes].astype(F32)
        step_w, end_w, cum_w = wide[0, :, lanes], wide[1, :, lanes], wide[2, :, lanes]
        carried = cum_w * (dot(c, eh) + dot(c, el))
        later = end_w * (dot(b, lh) + dot(b, ll))
        scaled = xs * step_w
        oh, ol = split(gs * cum_w)
        grad_c = grad_c + (dot(oh, eh, NT) + dot(oh, el, NT) + dot(ol, eh, NT))
        ih, il = split(scaled * end_w)
        grad_b = grad_b + (dot(ih, lh, NT) + dot(ih, ll, NT) + dot(il, lh, NT))
        du = du_ref[:, lanes] + later
        gx_ref[:, lanes] = (du * step_w).astype(BF16)
        last.append(jnp.sum(scaled * later, axis=0, keepdims=True)
                    + cum_w[span - 1:span] * jnp.sum(enter * leave, axis=0, keepdims=True))
        wide[2, :, lanes] = gs * carried
        du_ref[:, lanes] = du * xs
    mine = jnp.where(even, grad_b, grad_c)
    pair_s[...] = jnp.where(even, grad_c, grad_b)
    trade = send(pair_s, pair_r, s_pair, (), tensor=buddy)

    direct = gather_heads(du_ref[...])
    final = gather_heads(jnp.broadcast_to(jnp.concatenate(last, axis=1), (span, width)))
    dcum = row_part + gather_heads(wide[2]) - step * direct
    at_last = lax.broadcasted_iota(jnp.int32, (heads, span), 1) == span - 1
    dcum = dcum + jnp.where(at_last, final, 0.0)
    dlog = lax.dot_general(dcum, (rows >= cols).astype(F32), NN, precision=HIGHEST,
                           preferred_element_type=F32)
    rate_s[...] = jnp.broadcast_to(jnp.sum(dlog * log_decay, axis=1, keepdims=True), rate_s.shape)
    spreads = [send(rate_s, rate_r.at[apart - 1], s_rate, (apart - 1,),
                    seq=lax.rem(me + apart, seq_count)) for apart in range(1, seq_count)]
    gs_ref[...] = (direct + dlog * rate) * sigmoid
    trade.wait()
    gp_ref[...] = (mine + pair_r[...]).astype(BF16)
    summed = rate_s[...]
    for copy in spreads:
        copy.wait()
    for apart in range(1, seq_count):
        summed = summed + rate_r[apart - 1]
    gr_ref[...] = summed


def per_device(seq_count, inputs, projections, step_raw, rate_log, out_grad):
    _, span, width = inputs.shape
    heads = step_raw.shape[0]
    state = projections.shape[2]
    chunks = width // CHUNK
    half = chunks // 2
    levels = seq_count.bit_length() - 1
    dma = pltpu.SemaphoreType.DMA
    vmem = pl.BlockSpec(memory_space=pltpu.VMEM)
    tall = state + 8
    outs = pl.pallas_call(
        functools.partial(kernel, seq_count, width // heads),
        out_shape=(
            jax.ShapeDtypeStruct((span, width), BF16),
            jax.ShapeDtypeStruct((span, state), BF16),
            jax.ShapeDtypeStruct((heads, span), F32),
            jax.ShapeDtypeStruct((heads, 128), F32),
        ),
        in_specs=[vmem] * 5,
        out_specs=(vmem,) * 4,
        scratch_shapes=[
            pltpu.VMEM((span, state), BF16),
            pltpu.VMEM((chunks, 2, tall, CHUNK), F32),
            pltpu.VMEM((chunks, 2, tall, CHUNK), F32),
            pltpu.VMEM((max(levels - 2, 1), half, 2, tall, CHUNK), F32),
            pltpu.VMEM((max(levels - 2, 1), half, 2, tall, CHUNK), F32),
            pltpu.VMEM((half, tall, CHUNK), F32),
            pltpu.VMEM((half, tall, CHUNK), F32),
            pltpu.VMEM((chunks, 2, state, CHUNK), F32),
            pltpu.VMEM((3, span, width), F32),
            pltpu.VMEM((span, width), F32),
            pltpu.VMEM((span, state), F32),
            pltpu.VMEM((span, state), F32),
            pltpu.VMEM((heads, 128), F32),
            pltpu.VMEM((seq_count - 1, heads, 128), F32),
            dma((2,)),
            dma((2, half)),
            dma((2, half)),
            dma((2, max(levels - 2, 1), half)),
            dma((2, half)),
            dma((2, half)),
            dma((2,)),
            dma((2, seq_count - 1)),
        ],
        compiler_params=pltpu.CompilerParams(
            collective_id=0, has_side_effects=True, vmem_limit_bytes=56 * 2**20
        ),
    )(
        inputs.reshape(span, width),
        projections.reshape(span, state),
        step_raw.reshape(heads, span),
        jnp.broadcast_to(rate_log[:, None], (heads, 128)),
        out_grad.reshape(span, width),
    )
    gx, gp, gs, gr = outs
    return gx[None], gp[None], gs[:, None], gr[:, 0]


def solution(mesh):
    in_specs = (
        P(None, "seq", "tensor"),
        P(None, "seq", "tensor"),
        P("tensor", None, "seq"),
        P("tensor"),
        P(None, "seq", "tensor"),
    )
    out_specs = (
        P(None, "seq", "tensor"),
        P(None, "seq", "tensor"),
        P("tensor", None, "seq"),
        P("tensor"),
    )
    return jax.shard_map(
        functools.partial(per_device, mesh.shape["seq"]),
        mesh=mesh, in_specs=in_specs, out_specs=out_specs, check_vma=False,
    )
```

time: 184 us -> 59.9 us (0.33)
  waiting for transfers between devices: 55.2 us -> 0 us
  Pallas kernels: 0 us -> 53.3 us
  other arithmetic: 33.3 us -> 0 us
  blocking collectives: 27.7 us -> 0 us
  local copies, waits for them, and re-layouts: 28 us -> 5.63 us
  matrix products: 18.7 us -> 0 us
  between operations: 14.9 us -> 0.66 us
  starting transfers between devices: 4.72 us -> 0 us
    all_gather x2 -> x0, waiting for transfers between devices: 55.2 us -> none  [entering_2(): everything = jax.tree.map(lambda part: lax.all_gather(part, axis), value)]
    pallas_call x0 -> x1, Pallas kernels: none -> 53.3 us  [per_device(): pl.pallas_call(functools.partial(kernel, seq_count, width // heads), out_...]
    select_n x17 -> x0, other arithmetic: 23.5 us -> none  [the longest x16 23.4 us: step(): return jax.tree.map(lambda a, b: jnp.where(reached, a, b), new, before)]
    dot_general x11 -> x0, matrix products: 18.7 us -> none  [the longest x3 6.85 us: advance(): jnp.einsum('shj,sjhp,sjn->shpn', to_end, scaled_piece, inject_piece, prec...]
    mul x19 -> x0, local copies, waits for them, and re-layouts: 17.3 us -> none  [the longest x16 14.4 us: combine(): later[0][..., None, None] * earlier[1] + later[1]]
    unnamed x1 -> x0, blocking collectives: 14.4 us -> none
    psum x1 -> x0, blocking collectives: 13.3 us -> none  [per_device(): grad_rate = lax.psum(grad_rates, 'seq')]
    ppermute x2 -> x0, starting transfers between devices: 4.64 us -> none  [swapped(): return lax.ppermute(value, axis, pairs)]
  transfers between devices with their start and end apart: 4 -> 0, of which waited for: 2 -> 0; matrix products, arithmetic and copies ran while one was open for 25% -> 0% of each run, Pallas kernels for 0% -> 0%
where the time goes in v1:
time: 59.9 us; the launch traced here: 59.6 us
  Pallas kernels  53.3 us (89%)
  local copies, waits for them, and re-layouts  5.63 us (9%)
  between operations  0.66 us (1%)
    pallas_call x1, Pallas kernels, per_device(): pl.pallas_call(functools.partial(kernel, seq_count, width // heads), out_...  53.3 us
    unnamed x11, local copies, waits for them, and re-layouts  4.34 us

profile of v1, /device:TPU:0, one launch (start us, length us, event | category | flops | bytes accessed | tf_op | source)
XLA Modules:
  0.0 59.6 jit_solution(3768009483949315838)
XLA Ops:
  0.6 0.0 copy-start.3
  0.6 0.6 %copy-done.3 = f32[16]{0:T(128)S(1)} copy-done((f32[16]{0:T(128)S(1)}, f32[16]{0:T(128)}, u32[]{:S(2)}) %copy-start.3) | copy-done | bytes 88
  1.3 0.7 %broadcast_in_dim.15.rate_ref = f32[16,128]{1,0:T(8,128)} broadcast(f32[16]{0:T(128)S(1)} %copy-done.3), dimensions={0} | broadcast | bytes 8256 | tf_op jit(solution)/shard_map/broadcast_in_dim | solution.py:321
  2.0 53.3 %shard_map.84 = (bf16[128,1024]{1,0:T(8,128)(2,1)}, bf16[128,256]{1,0:T(8,128)(2,1)}, f32[16,128]{1,0:T(8,128)}, f32[16,128]{1,0:T(8,128)}) custom-call(bf16[128,1024]{1,0:T(8,128)(2,1)} %bitcast.9, bf16[128,256]{1,0:T(8,128)(2,1)} %bitcast.12, f32[16,128]{1,0:T(8,128)} %bitcast.14, f32[16,128]{1,0:T(8,128)} %broadcast_in_dim.15.rate_ref, ...), custom_call_target="tpu_custom_call" | custom-call | tf_op jit(solution)/shard_map/pallas_call | solution.py:280
  55.3 0.0 copy-start.2
  55.3 0.7 %copy-done.2 = f32[16,128]{1,0:T(8,128)S(1)} copy-done((f32[16,128]{1,0:T(8,128)S(1)}, f32[16,128]{1,0:T(8,128)}, u32[]{:S(2)}) %copy-start.2) | copy-done | bytes 8216
  56.0 0.6 %slice_reduce_fusion = f32[16]{0:T(128)} fusion(f32[16,128]{1,0:T(8,128)S(1)} %copy-done.2), kind=kLoop, calls=%fused_computation | loop fusion | bytes 128 | tf_op jit(solution)/shard_map/slice | solution.py:325
  56.6 0.0 copy-start
  56.6 1.7 %copy.14 = bf16[1,128,1024]{2,1,0:T(8,128)(2,1)} copy(bf16[1,128,1024]{2,1,0:T(8,128)(2,1)} %bitcast.11) | data formatting | bytes 524288
  58.3 0.0 copy-done
  58.3 0.0 copy-start.1
  58.3 0.6 %copy.15 = bf16[1,128,256]{2,1,0:T(8,128)(2,1)} copy(bf16[1,128,256]{2,1,0:T(8,128)(2,1)S(1)} %bitcast.13) | data formatting | bytes 131072
  59.0 0.1 copy-done.1
  59.0 0.6 %copy.16 = f32[16,1,128]{2,1,0:T(1,128)} copy(f32[16,1,128]{2,1,0:T(1,128)S(1)} %bitcast.15) | data formatting | bytes 16384
Async XLA Ops:
  0.6 0.7 %copy-start.3 = (f32[16]{0:T(128)S(1)}, f32[16]{0:T(128)}, u32[]{:S(2)}) copy-start(f32[16]{0:T(128)} %param.8) | copy-start | bytes 196
  55.3 0.7 %copy-start.2 = (f32[16,128]{1,0:T(8,128)S(1)}, f32[16,128]{1,0:T(8,128)}, u32[]{:S(2)}) copy-start(f32[16,128]{1,0:T(8,128)} %get-tuple-element.11) | copy-start | bytes 24580
  56.6 1.7 %copy-start = (bf16[128,256]{1,0:T(8,128)(2,1)S(1)}, bf16[128,256]{1,0:T(8,128)(2,1)}, u32[]{:S(2)}) copy-start(bf16[128,256]{1,0:T(8,128)(2,1)} %get-tuple-element.9) | copy-start | bytes 196612
  58.3 0.7 %copy-start.1 = (f32[16,128]{1,0:T(8,128)S(1)}, f32[16,128]{1,0:T(8,128)}, u32[]{:S(2)}) copy-start(f32[16,128]{1,0:T(8,128)} %get-tuple-element.10) | copy-start | bytes 24580

commit v2 on v1

--- a/solution.py
+++ b/solution.py
@@ -25,11 +25,18 @@
     return high, (a - high.astype(F32)).astype(BF16)
 
 
+def softplus(raw):
+    small = jnp.exp(-jnp.abs(raw))
+    one = 1.0 + small
+    log1p = jnp.where(one == 1.0, small, jnp.log(one) * small / jnp.where(one == 1.0, 1.0, one - 1.0))
+    return jnp.maximum(raw, 0.0) + log1p
+
+
 def kernel(seq_count, head_width, x_ref, proj_ref, raw_ref, rate_ref, g_ref,
            gx_ref, gp_ref, gs_ref, gr_ref,
-           other, local, near, tots, totr, lasts, lastr, passed, wide, du_ref,
-           pair_s, pair_r, rate_s, rate_r,
-           s_other, s_near, s_far, s_tot, s_last, s_pass, s_pair, s_rate):
+           other, stage, quad, pairs, raws, parts, outer, tots, totr, lasts, lastr, give, passed,
+           wide, du_ref, pair_s, pair_r, rate_s, rate_r,
+           s_other, s_first, s_second, s_proj, s_raw, s_tot, s_last, s_pass, s_pair, s_rate):
     span, width = x_ref.shape
     heads = raw_ref.shape[0]
     state = proj_ref.shape[1]
@@ -62,13 +69,28 @@
         return copy
 
     swap = send(proj_ref, other, s_other, (), tensor=buddy)
+    place = lax.rem(me, 4)
+    base = me - place
+    across = lax.rem(place // 2, 2)
+    last_up = partner(levels - 1)[1]
+    urgent = last_up
+    side = width // 2
+    raws[place] = raw_ref[...]
+    for part in range(2):
+        stage[part, 0] = x_ref[:, part * side:(part + 1) * side]
+        stage[part, 1] = g_ref[:, part * side:(part + 1) * side]
+    peers = []
+    for flip in (2, 3, 1):
+        there = place + (1 - 2 * lax.rem(place, 2)) * (flip % 2) + (2 - 4 * across) * (flip // 2)
+        peers.append((flip - 1, base + there, lax.rem(there, 2)))
+    first = [(send(raws.at[place], raws.at[place], s_raw, (i,), seq=to),
+              send(stage.at[half_of, urgent], quad.at[place, urgent], s_first, (i,), seq=to))
+             for i, to, half_of in peers]
+    quad[place] = stage[core]
 
     raw = raw_ref[...]
-    small = jnp.exp(-jnp.abs(raw))
-    one = 1.0 + small
-    log1p = jnp.where(one == 1.0, small, jnp.log(one) * small / jnp.where(one == 1.0, 1.0, one - 1.0))
-    step = jnp.maximum(raw, 0.0) + log1p
-    sigmoid = jnp.where(raw >= 0, 1.0, small) / one
+    step = softplus(raw)
+    sigmoid = 1.0 / (1.0 + jnp.exp(-raw))
     rate = -jnp.exp(rate_ref[:, 0:1])
     log_decay = rate * step
     rows = lax.broadcasted_iota(jnp.int32, (span, span), 0)
@@ -82,12 +104,18 @@
     spread = ((at_col >= at_row) & (at_col < at_row + head_width)).astype(F32).astype(BF16)
     spread3 = jnp.concatenate([spread, spread, spread], axis=0)
 
-    def widen(a):
+    few_spread = spread[:heads // 2, :width // 2]
+    few_spread3 = jnp.concatenate([few_spread, few_spread, few_spread], axis=0)
+
+    def widen(a, by=spread3):
         high = a.astype(BF16)
         rest = a - high.astype(F32)
         mid = rest.astype(BF16)
         low = (rest - mid.astype(F32)).astype(BF16)
-        return dot(jnp.concatenate([high, mid, low], axis=0), spread3, TN)
+        return dot(jnp.concatenate([high, mid, low], axis=0), by, TN)
+
+    def widen_half(a):
+        return widen(a, few_spread3)
 
     def gather_heads(a):
         high = a.astype(BF16)
@@ -103,55 +131,11 @@
     b = jnp.where(even, own, theirs).astype(BF16)
     c = jnp.where(even, theirs, own).astype(BF16)
 
-    for q in range(chunks):
-        lanes = slice(q * CHUNK, (q + 1) * CHUNK)
-        inj = x_ref[:, lanes].astype(F32) * wide[0, :, lanes] * wide[1, :, lanes]
-        out = g_ref[:, lanes].astype(F32) * wide[2, :, lanes]
-        high, low = split(inj)
-        local[q, 0, :state] = dot(b, high, TN) + dot(b, low, TN)
-        high, low = split(out)
-        local[q, 1, :state] = dot(c, high, TN) + dot(c, low, TN)
-        decay = jnp.broadcast_to(wide[2, span - 1:span, lanes], (8, CHUNK))
-        local[q, 0, state:] = decay
-        local[q, 1, state:] = decay
-
-    mate, _ = partner(0)
-    close = [send(local.at[(1 - core) * half + k], near.at[(1 - core) * half + k], s_near, (k,), seq=mate)
-             for k in range(half)]
-    rest = [send(local.at[core * half + k, core], near.at[core * half + k, core], s_far, (k,), seq=mate)
-            for k in range(half)]
-
-    is_up = core == 1
-
-    def merge(up, f_own, r_own, d_own, f_in, r_in, d_in):
-        f = jnp.where(up, 1.0, d_in) * f_own + jnp.where(up, d_own, 1.0) * f_in
-        r = jnp.where(up, d_in, 1.0) * r_own + jnp.where(up, 1.0, d_own) * r_in
-        return f, r, d_own * d_in
-
-    sent = {}
-
-    def put(level, k, f, r, d):
-        target, upper = partner(level)
-        d8 = jnp.broadcast_to(d, (8, CHUNK))
-        if level == levels - 1:
-            lasts[k, :state] = jnp.where(upper == 1, r, f)
-            lasts[k, state:] = d8
-            sent[level, k] = send(lasts.at[k], lastr.at[k], s_last, (k,), seq=target)
-        else:
-            tots[level - 1, k, 0, :state] = f
-            tots[level - 1, k, 1, :state] = r
-            tots[level - 1, k, 0, state:] = d8
-            tots[level - 1, k, 1, state:] = d8
-            sent[level, k] = send(tots.at[level - 1, k], totr.at[level - 1, k], s_tot,
-                                  (level - 1, k), seq=target)
-
-    for k in range(half):
-        close[k].wait()
-        q = core * half + k
-        f, r, d = merge(is_up, local[q, 0, :state], local[q, 1, :state], local[q, 0, state:state + 1],
-                        near[core * half + k, 0, :state], near[core * half + k, 1, :state],
-                        near[core * half + k, 0, state:state + 1])
-        put(1, k, f, r, d)
+    pairs[place, 0] = b
+    pairs[place, 1] = c
+    second = [(send(pairs.at[place], pairs.at[place], s_proj, (i,), seq=to),
+               send(stage.at[half_of, 1 - urgent], quad.at[place, 1 - urgent], s_second, (i,), seq=to))
+              for i, to, half_of in peers]
 
     scores = dot(b, c, NT)
     total_scores = jnp.zeros((span, span), F32)
@@ -182,49 +166,131 @@
     grad_b = dot(high, c) + dot(low, c)
     grad_c = dot(high, b, TN) + dot(low, b, TN)
 
-    zero = jnp.zeros((state, CHUNK), F32)
+    for copies in first:
+        copies[0].wait()
+    few = heads // 2
+    wide_step, wide_cum, decays = [], [], []
+    rate_half = jnp.where(core == 0, rate[:few], rate[few:])
+    for r in range(4):
+        step_r = softplus(jnp.where(core == 0, raws[r, :few], raws[r, few:]))
+        cum_r = lax.dot_general(rate_half * step_r, causal.astype(F32), NN, precision=HIGHEST,
+                                preferred_element_type=F32)
+        wide_step.append((step_r, cum_r))
+        decays.append(widen_half(jnp.exp(cum_r))[span - 1:span])
+
+    def block_state(r, which):
+        step_r, cum_r = wide_step[r]
+        weight = jnp.where(which == 0, step_r * jnp.exp(cum_r[:, span - 1:span] - cum_r), jnp.exp(cum_r))
+        high, low = split(quad[r, which].astype(F32) * widen_half(weight))
+        basis = pairs[r, which]
+        parts[r, which] = dot(basis, high, TN) + dot(basis, low, TN)
+
+    def cut(row, k):
+        return row[:, k * CHUNK:(k + 1) * CHUNK]
+
+    def join(which, r, k):
+        lanes = slice(k * CHUNK, (k + 1) * CHUNK)
+        d0, d1 = cut(decays[r], k), cut(decays[r + 1], k)
+        return (jnp.where(which == 0, d1, 1.0) * parts[r, which, :, lanes]
+                + jnp.where(which == 0, 1.0, d0) * parts[r + 1, which, :, lanes])
+
+    def whole(which, k):
+        d01 = cut(decays[0], k) * cut(decays[1], k)
+        d23 = cut(decays[2], k) * cut(decays[3], k)
+        return (jnp.where(which == 0, d23, 1.0) * join(which, 0, k)
+                + jnp.where(which == 0, 1.0, d01) * join(which, 2, k))
+
+    def all_decay(k):
+        return (cut(decays[0], k) * cut(decays[1], k)) * (cut(decays[2], k) * cut(decays[3], k))
+
+    def merge(up, f_own, r_own, d_own, f_in, r_in, d_in):
+        f = jnp.where(up, 1.0, d_in) * f_own + jnp.where(up, d_own, 1.0) * f_in
+        r = jnp.where(up, d_in, 1.0) * r_own + jnp.where(up, 1.0, d_own) * r_in
+        return f, r, d_own * d_in
+
+    sent = {}
+
+    def put_last(k, value):
+        lasts[k] = value
+        sent[levels - 1, k] = send(lasts.at[k], lastr.at[k], s_last, (k,), seq=partner(levels - 1)[0])
+
+    def put(level, k, f, r, d):
+        if level == levels - 1:
+            put_last(k, jnp.where(last_up == 1, r, f))
+        else:
+            d8 = jnp.broadcast_to(d, (8, CHUNK))
+            for i, value in enumerate((f, r)):
+                tots[level - 2, k, i, :state] = value
+                tots[level - 2, k, i, state:] = d8
+            sent[level, k] = send(tots.at[level - 2, k], totr.at[level - 2, k], s_tot,
+                                  (level - 2, k), seq=partner(level)[0])
+
+    for copies in first:
+        copies[1].wait()
+    for copies in second:
+        copies[0].wait()
+    for r in range(4):
+        block_state(r, urgent)
+    if levels == 3:
+        for k in range(half):
+            put_last(k, whole(urgent, k))
+    for copies in second:
+        copies[1].wait()
+    for r in range(4):
+        block_state(r, 1 - urgent)
+    if levels > 3:
+        for k in range(half):
+            put(2, k, whole(0, k), whole(1, k), all_decay(k))
+        outer[...] = jnp.zeros_like(outer)
+
+    mate, _ = partner(0)
     ones = jnp.ones((1, CHUNK), F32)
     dp, dq = [ones] * half, [ones] * half
-    for k in range(half):
-        passed[core * half + k, 0] = zero
-        passed[core * half + k, 1] = zero
     moved = []
-    for level in range(1, levels):
-        _, upper = partner(level)
-        up = upper == 1
+    for level in range(2, levels):
+        up = partner(level)[1] == 1
         for k in range(half):
-            sent[level, k].wait()
-            q = core * half + k
-            if level == levels - 1:
-                got = lastr[k, :state]
-                before, after = passed[q, 0], passed[q, 1]
-                passed[q, 0] = before + jnp.where(up, dp[k], 0.0) * got
-                passed[q, 1] = after + jnp.where(up, 0.0, dq[k]) * got
-                moved.append(send(passed.at[q], passed.at[q], s_pass, (k,), seq=mate))
-            else:
-                at = level - 1
+            if level < levels - 1:
+                sent[level, k].wait()
+                at = level - 2
                 f_in, r_in = totr[at, k, 0, :state], totr[at, k, 1, :state]
                 d_in = totr[at, k, 0, state:state + 1]
-                passed[q, 0] = passed[q, 0] + jnp.where(up, dp[k], 0.0) * f_in
-                passed[q, 1] = passed[q, 1] + jnp.where(up, 0.0, dq[k]) * r_in
+                outer[k, 0] = outer[k, 0] + jnp.where(up, dp[k], 0.0) * f_in
+                outer[k, 1] = outer[k, 1] + jnp.where(up, 0.0, dq[k]) * r_in
                 dp[k] = dp[k] * jnp.where(up, d_in, 1.0)
                 dq[k] = dq[k] * jnp.where(up, 1.0, d_in)
                 f, r, d = merge(up, tots[at, k, 0, :state], tots[at, k, 1, :state],
                                 tots[at, k, 0, state:state + 1], f_in, r_in, d_in)
                 put(level + 1, k, f, r, d)
-    for copy in rest + moved:
+                continue
+            right = across == 1
+            lanes = slice(k * CHUNK, (k + 1) * CHUNK)
+            d0, d1, d2, d3 = (cut(row, k) for row in decays)
+            near0, near1 = jnp.where(right, d2, d0), jnp.where(right, d3, d1)
+            enter0 = jnp.where(right, join(0, 0, k), 0.0)
+            leave1 = jnp.where(right, 0.0, join(1, 2, k))
+            sent[level, k].wait()
+            got = lastr[k]
+            before, after = jnp.where(up, dp[k], 0.0) * got, jnp.where(up, 0.0, dq[k]) * got
+            if levels > 3:
+                before, after = before + outer[k, 0], after + outer[k, 1]
+            enter0 = enter0 + jnp.where(right, d0 * d1, 1.0) * before
+            leave1 = leave1 + jnp.where(right, 1.0, d2 * d3) * after
+            enter1 = near0 * enter0 + parts[2 * across, 0, :, lanes]
+            leave0 = near1 * leave1 + parts[2 * across + 1, 1, :, lanes]
+            odd = core == 1
+            give[k, 0] = jnp.where(odd, enter0, enter1)
+            give[k, 1] = jnp.where(odd, leave0, leave1)
+            moved.append(send(give.at[k], passed.at[core * half + k], s_pass, (k,), seq=mate))
+            passed[core * half + k, 0] = jnp.where(odd, enter1, enter0)
+            passed[core * half + k, 1] = jnp.where(odd, leave1, leave0)
+    for copy in moved:
         copy.wait()
 
-    dcum = row_part
     last = []
-    taken = []
     for q in range(chunks):
         lanes = slice(q * CHUNK, (q + 1) * CHUNK)
-        before, after = passed[q, 0], passed[q, 1]
-        side = near[q, 1 - core]
-        joined = side[:state] + side[state:state + 1] * jnp.where(is_up, before, after)
-        enter = jnp.where(is_up, joined, before)
-        leave = jnp.where(is_up, after, joined)
+        enter, leave = passed[q, 0], passed[q, 1]
         eh, el = split(enter)
         lh, ll = split(leave)
         xs, gs = x_ref[:, lanes].astype(F32), g_ref[:, lanes].astype(F32)
@@ -289,12 +355,17 @@
         out_specs=(vmem,) * 4,
         scratch_shapes=[
             pltpu.VMEM((span, state), BF16),
-            pltpu.VMEM((chunks, 2, tall, CHUNK), F32),
-            pltpu.VMEM((chunks, 2, tall, CHUNK), F32),
-            pltpu.VMEM((max(levels - 2, 1), half, 2, tall, CHUNK), F32),
-            pltpu.VMEM((max(levels - 2, 1), half, 2, tall, CHUNK), F32),
-            pltpu.VMEM((half, tall, CHUNK), F32),
-            pltpu.VMEM((half, tall, CHUNK), F32),
+            pltpu.VMEM((2, 2, span, width // 2), BF16),
+            pltpu.VMEM((4, 2, span, width // 2), BF16),
+            pltpu.VMEM((4, 2, span, state), BF16),
+            pltpu.VMEM((4, heads, span), F32),
+            pltpu.VMEM((4, 2, state, width // 2), F32),
+            pltpu.VMEM((half, 2, state, CHUNK), F32),
+            pltpu.VMEM((max(levels - 3, 1), half, 2, tall, CHUNK), F32),
+            pltpu.VMEM((max(levels - 3, 1), half, 2, tall, CHUNK), F32),
+            pltpu.VMEM((half, state, CHUNK), F32),
+            pltpu.VMEM((half, state, CHUNK), F32),
+            pltpu.VMEM((half, 2, state, CHUNK), F32),
             pltpu.VMEM((chunks, 2, state, CHUNK), F32),
             pltpu.VMEM((3, span, width), F32),
             pltpu.VMEM((span, width), F32),
@@ -303,9 +374,11 @@
             pltpu.VMEM((heads, 128), F32),
             pltpu.VMEM((seq_count - 1, heads, 128), F32),
             dma((2,)),
-            dma((2, half)),
-            dma((2, half)),
-            dma((2, max(levels - 2, 1), half)),
+            dma((2, 3)),
+            dma((2, 3)),
+            dma((2, 3)),
+            dma((2, 3)),
+            dma((2, max(levels - 3, 1), half)),
             dma((2, half)),
             dma((2, half)),
             dma((2,)),

time: 59.9 us -> 52.1 us (0.87)
  Pallas kernels: 53.3 us -> 45.6 us
    pallas_call x1, Pallas kernels: 53.3 us -> 45.6 us  [per_device(): pl.pallas_call(functools.partial(kernel, seq_count, width // heads), out_...]
where the time goes in v2:
time: 52.1 us; the launch traced here: 51.9 us
  Pallas kernels  45.6 us (88%)
  local copies, waits for them, and re-layouts  5.63 us (11%)
  between operations  0.66 us (1%)
    pallas_call x1, Pallas kernels, per_device(): pl.pallas_call(functools.partial(kernel, seq_count, width // heads), out_...  45.6 us
    unnamed x11, local copies, waits for them, and re-layouts  4.34 us

profile of v2, /device:TPU:0, one launch (start us, length us, event | category | flops | bytes accessed | tf_op | source)
XLA Modules:
  0.0 51.9 jit_solution(13142094658649828897)
XLA Ops:
  0.6 0.0 copy-start.3
  0.6 0.6 %copy-done.3 = f32[16]{0:T(128)S(1)} copy-done((f32[16]{0:T(128)S(1)}, f32[16]{0:T(128)}, u32[]{:S(2)}) %copy-start.3) | copy-done | bytes 88
  1.3 0.7 %broadcast_in_dim.15.rate_ref = f32[16,128]{1,0:T(8,128)} broadcast(f32[16]{0:T(128)S(1)} %copy-done.3), dimensions={0} | broadcast | bytes 8256 | tf_op jit(solution)/shard_map/broadcast_in_dim | solution.py:394
  2.0 45.6 %shard_map.84 = (bf16[128,1024]{1,0:T(8,128)(2,1)}, bf16[128,256]{1,0:T(8,128)(2,1)}, f32[16,128]{1,0:T(8,128)}, f32[16,128]{1,0:T(8,128)}) custom-call(bf16[128,1024]{1,0:T(8,128)(2,1)} %bitcast.9, bf16[128,256]{1,0:T(8,128)(2,1)} %bitcast.12, f32[16,128]{1,0:T(8,128)} %bitcast.14, f32[16,128]{1,0:T(8,128)} %broadcast_in_dim.15.rate_ref, ...), custom_call_target="tpu_custom_call" | custom-call | tf_op jit(solution)/shard_map/pallas_call | solution.py:346
  47.6 0.0 copy-start.2
  47.6 0.7 %copy-done.2 = f32[16,128]{1,0:T(8,128)S(1)} copy-done((f32[16,128]{1,0:T(8,128)S(1)}, f32[16,128]{1,0:T(8,128)}, u32[]{:S(2)}) %copy-start.2) | copy-done | bytes 8216
  48.3 0.6 %slice_reduce_fusion = f32[16]{0:T(128)} fusion(f32[16,128]{1,0:T(8,128)S(1)} %copy-done.2), kind=kLoop, calls=%fused_computation | loop fusion | bytes 128 | tf_op jit(solution)/shard_map/slice | solution.py:398
  48.9 0.0 copy-start
  48.9 1.7 %copy.14 = bf16[1,128,1024]{2,1,0:T(8,128)(2,1)} copy(bf16[1,128,1024]{2,1,0:T(8,128)(2,1)} %bitcast.11) | data formatting | bytes 524288
  50.6 0.0 copy-done
  50.6 0.0 copy-start.1
  50.6 0.6 %copy.15 = bf16[1,128,256]{2,1,0:T(8,128)(2,1)} copy(bf16[1,128,256]{2,1,0:T(8,128)(2,1)S(1)} %bitcast.13) | data formatting | bytes 131072
  51.2 0.1 copy-done.1
  51.3 0.6 %copy.16 = f32[16,1,128]{2,1,0:T(1,128)} copy(f32[16,1,128]{2,1,0:T(1,128)S(1)} %bitcast.15) | data formatting | bytes 16384
Async XLA Ops:
  0.6 0.7 %copy-start.3 = (f32[16]{0:T(128)S(1)}, f32[16]{0:T(128)}, u32[]{:S(2)}) copy-start(f32[16]{0:T(128)} %param.8) | copy-start | bytes 196
  47.6 0.7 %copy-start.2 = (f32[16,128]{1,0:T(8,128)S(1)}, f32[16,128]{1,0:T(8,128)}, u32[]{:S(2)}) copy-start(f32[16,128]{1,0:T(8,128)} %get-tuple-element.11) | copy-start | bytes 24580
  48.9 1.7 %copy-start = (bf16[128,256]{1,0:T(8,128)(2,1)S(1)}, bf16[128,256]{1,0:T(8,128)(2,1)}, u32[]{:S(2)}) copy-start(bf16[128,256]{1,0:T(8,128)(2,1)} %get-tuple-element.9) | copy-start | bytes 196612
  50.6 0.7 %copy-start.1 = (f32[16,128]{1,0:T(8,128)S(1)}, f32[16,128]{1,0:T(8,128)}, u32[]{:S(2)}) copy-start(f32[16,128]{1,0:T(8,128)} %get-tuple-element.10) | copy-start | bytes 24580

commit v3 on v2

--- a/solution.py
+++ b/solution.py
@@ -11,6 +11,7 @@
 HIGHEST = lax.Precision.HIGHEST
 F32, BF16 = jnp.float32, jnp.bfloat16
 CHUNK = 256
+EARLY = 2
 NT = (((1,), (1,)), ((), ()))
 TN = (((0,), (0,)), ((), ()))
 NN = (((1,), (0,)), ((), ()))
@@ -74,24 +75,35 @@
     across = lax.rem(place // 2, 2)
     last_up = partner(levels - 1)[1]
     urgent = last_up
-    side = width // 2
     raws[place] = raw_ref[...]
-    for part in range(2):
-        stage[part, 0] = x_ref[:, part * side:(part + 1) * side]
-        stage[part, 1] = g_ref[:, part * side:(part + 1) * side]
+    for q in range(chunks):
+        lanes = slice(q * CHUNK, (q + 1) * CHUNK)
+        stage[q // half, q % half, 0] = x_ref[:, lanes]
+        stage[q // half, q % half, 1] = g_ref[:, lanes]
     peers = []
     for flip in (2, 3, 1):
         there = place + (1 - 2 * lax.rem(place, 2)) * (flip % 2) + (2 - 4 * across) * (flip // 2)
         peers.append((flip - 1, base + there, lax.rem(there, 2)))
-    first = [(send(raws.at[place], raws.at[place], s_raw, (i,), seq=to),
-              send(stage.at[half_of, urgent], quad.at[place, urgent], s_first, (i,), seq=to))
-             for i, to, half_of in peers]
+    news = [send(raws.at[place], raws.at[place], s_raw, (i,), seq=to) for i, to, _ in peers]
+
+    def share(k, which, sems):
+        return [send(stage.at[half_of, k, which], quad.at[place, k, which], sems, (k, i), seq=to)
+                for i, to, half_of in peers]
+
+    def share_basis(which, at):
+        return [send(pairs.at[place, which], pairs.at[place, which], s_proj, (at, i), seq=to)
+                for i, to, _ in peers]
+
+    first, second = [share(0, urgent, s_first)], []
     quad[place] = stage[core]
 
     raw = raw_ref[...]
     step = softplus(raw)
     sigmoid = 1.0 / (1.0 + jnp.exp(-raw))
-    rate = -jnp.exp(rate_ref[:, 0:1])
+    head_row = lax.broadcasted_iota(jnp.int32, (heads, heads), 0)
+    diagonal = head_row == lax.broadcasted_iota(jnp.int32, (heads, heads), 1)
+    rate_row = jnp.broadcast_to(-jnp.exp(rate_ref[...]), (heads, heads))
+    rate = jnp.sum(jnp.where(diagonal, rate_row, 0.0), axis=1, keepdims=True)
     log_decay = rate * step
     rows = lax.broadcasted_iota(jnp.int32, (span, span), 0)
     cols = lax.broadcasted_iota(jnp.int32, (span, span), 1)
@@ -133,9 +145,10 @@
 
     pairs[place, 0] = b
     pairs[place, 1] = c
-    second = [(send(pairs.at[place], pairs.at[place], s_proj, (i,), seq=to),
-               send(stage.at[half_of, 1 - urgent], quad.at[place, 1 - urgent], s_second, (i,), seq=to))
-              for i, to, half_of in peers]
+    basis_first = share_basis(urgent, 0)
+    first += [share(k, urgent, s_first) for k in range(1, half)]
+    basis_second = share_basis(1 - urgent, 1)
+    second = [share(k, 1 - urgent, s_second) for k in range(half)]
 
     scores = dot(b, c, NT)
     total_scores = jnp.zeros((span, span), F32)
@@ -144,30 +157,29 @@
     lane = lax.broadcasted_iota(jnp.int32, (span, 128), 1)
     per = 128 // head_width
     from_rows = []
-    for p in range(width // 128):
-        lanes = slice(p * 128, (p + 1) * 128)
-        xs, gs = x_ref[:, lanes], g_ref[:, lanes]
-        grown = jnp.zeros((span, 128), F32)
-        for part in range(per):
-            h = p * per + part
-            mine = (lane >= part * head_width) & (lane < (part + 1) * head_width)
-            inner = dot(jnp.where(mine, xs.astype(F32), 0.0).astype(BF16), gs, NT)
-            gap = cum[h:h + 1, :] - cum_t[:, h:h + 1]
-            fade = jnp.exp(jnp.where(causal, gap, -1e30))
-            weight = fade * scores
-            flow = inner * step_t[:, h:h + 1]
-            total_scores = total_scores + flow * fade
-            from_rows.append(jnp.sum(flow * weight, axis=0, keepdims=True))
-            high, low = split(weight)
-            grown = jnp.where(mine, dot(high, gs) + dot(low, gs), grown)
-        du_ref[:, lanes] = grown
-    row_part = jnp.concatenate(from_rows, axis=0)
-    high, low = split(total_scores)
-    grad_b = dot(high, c) + dot(low, c)
-    grad_c = dot(high, b, TN) + dot(low, b, TN)
-
-    for copies in first:
-        copies[0].wait()
+    def inside(first_pair, end_pair, total_scores):
+        for p in range(first_pair, end_pair):
+            lanes = slice(p * 128, (p + 1) * 128)
+            xs, gs = x_ref[:, lanes], g_ref[:, lanes]
+            grown = jnp.zeros((span, 128), F32)
+            for part in range(per):
+                h = p * per + part
+                mine = (lane >= part * head_width) & (lane < (part + 1) * head_width)
+                inner = dot(jnp.where(mine, xs.astype(F32), 0.0).astype(BF16), gs, NT)
+                gap = cum[h:h + 1, :] - cum_t[:, h:h + 1]
+                fade = jnp.exp(jnp.where(causal, gap, -1e30))
+                weight = fade * scores
+                flow = inner * step_t[:, h:h + 1]
+                total_scores = total_scores + flow * fade
+                from_rows.append(jnp.sum(flow * weight, axis=0, keepdims=True))
+                high, low = split(weight)
+                grown = jnp.where(mine, dot(high, gs) + dot(low, gs), grown)
+            du_ref[:, lanes] = grown
+        return total_scores
+
+    total_scores = inside(0, EARLY, total_scores)
+    for copy in news:
+        copy.wait()
     few = heads // 2
     wide_step, wide_cum, decays = [], [], []
     rate_half = jnp.where(core == 0, rate[:few], rate[few:])
@@ -178,12 +190,18 @@
         wide_step.append((step_r, cum_r))
         decays.append(widen_half(jnp.exp(cum_r))[span - 1:span])
 
-    def block_state(r, which):
+    def weigh(r, which):
         step_r, cum_r = wide_step[r]
-        weight = jnp.where(which == 0, step_r * jnp.exp(cum_r[:, span - 1:span] - cum_r), jnp.exp(cum_r))
-        high, low = split(quad[r, which].astype(F32) * widen_half(weight))
+        return widen_half(jnp.where(which == 0, step_r * jnp.exp(cum_r[:, span - 1:span] - cum_r),
+                                    jnp.exp(cum_r)))
+
+    urgent_weights = [weigh(r, urgent) for r in range(4)]
+
+    def block_state(r, which, k, weight):
+        lanes = slice(k * CHUNK, (k + 1) * CHUNK)
+        high, low = split(quad[r, k, which].astype(F32) * weight[:, lanes])
         basis = pairs[r, which]
-        parts[r, which] = dot(basis, high, TN) + dot(basis, low, TN)
+        parts[r, which, :, lanes] = dot(basis, high, TN) + dot(basis, low, TN)
 
     def cut(row, k):
         return row[:, k * CHUNK:(k + 1) * CHUNK]
@@ -225,19 +243,28 @@
             sent[level, k] = send(tots.at[level - 2, k], totr.at[level - 2, k], s_tot,
                                   (level - 2, k), seq=partner(level)[0])
 
-    for copies in first:
-        copies[1].wait()
-    for copies in second:
-        copies[0].wait()
-    for r in range(4):
-        block_state(r, urgent)
-    if levels == 3:
-        for k in range(half):
+    for copy in basis_first:
+        copy.wait()
+    for k in range(half):
+        for copy in first[k]:
+            copy.wait()
+        for r in range(4):
+            block_state(r, urgent, k, urgent_weights[r])
+        if levels == 3:
             put_last(k, whole(urgent, k))
-    for copies in second:
-        copies[1].wait()
-    for r in range(4):
-        block_state(r, 1 - urgent)
+    total_scores = inside(EARLY, width // 128, total_scores)
+    row_part = jnp.concatenate(from_rows, axis=0)
+    high, low = split(total_scores)
+    grad_b = dot(high, c) + dot(low, c)
+    grad_c = dot(high, b, TN) + dot(low, b, TN)
+    weights = [weigh(r, 1 - urgent) for r in range(4)]
+    for copy in basis_second:
+        copy.wait()
+    for k in range(half):
+        for copy in second[k]:
+            copy.wait()
+        for r in range(4):
+            block_state(r, 1 - urgent, k, weights[r])
     if levels > 3:
         for k in range(half):
             put(2, k, whole(0, k), whole(1, k), all_decay(k))
@@ -330,7 +357,7 @@
         copy.wait()
     for apart in range(1, seq_count):
         summed = summed + rate_r[apart - 1]
-    gr_ref[...] = summed
+    gr_ref[...] = jnp.sum(jnp.where(diagonal, summed[:, :heads], 0.0), axis=0, keepdims=True)
 
 
 def per_device(seq_count, inputs, projections, step_raw, rate_log, out_grad):
@@ -349,14 +376,14 @@
             jax.ShapeDtypeStruct((span, width), BF16),
             jax.ShapeDtypeStruct((span, state), BF16),
             jax.ShapeDtypeStruct((heads, span), F32),
-            jax.ShapeDtypeStruct((heads, 128), F32),
+            jax.ShapeDtypeStruct((1, heads), F32),
         ),
         in_specs=[vmem] * 5,
         out_specs=(vmem,) * 4,
         scratch_shapes=[
             pltpu.VMEM((span, state), BF16),
-            pltpu.VMEM((2, 2, span, width // 2), BF16),
-            pltpu.VMEM((4, 2, span, width // 2), BF16),
+            pltpu.VMEM((2, half, 2, span, CHUNK), BF16),
+            pltpu.VMEM((4, half, 2, span, CHUNK), BF16),
             pltpu.VMEM((4, 2, span, state), BF16),
             pltpu.VMEM((4, heads, span), F32),
             pltpu.VMEM((4, 2, state, width // 2), F32),
@@ -374,9 +401,9 @@
             pltpu.VMEM((heads, 128), F32),
             pltpu.VMEM((seq_count - 1, heads, 128), F32),
             dma((2,)),
-            dma((2, 3)),
-            dma((2, 3)),
-            dma((2, 3)),
+            dma((2, half, 3)),
+            dma((2, half, 3)),
+            dma((2, 2, 3)),
             dma((2, 3)),
             dma((2, max(levels - 3, 1), half)),
             dma((2, half)),
@@ -391,11 +418,11 @@
         inputs.reshape(span, width),
         projections.reshape(span, state),
         step_raw.reshape(heads, span),
-        jnp.broadcast_to(rate_log[:, None], (heads, 128)),
+        rate_log.reshape(1, heads),
         out_grad.reshape(span, width),
     )
     gx, gp, gs, gr = outs
-    return gx[None], gp[None], gs[:, None], gr[:, 0]
+    return gx[None], gp[None], gs[:, None], gr[0]
 
 
 def solution(mesh):

time: 52.1 us -> 40.8 us (0.78)
  Pallas kernels: 45.6 us -> 36.4 us
  local copies, waits for them, and re-layouts: 5.63 us -> 3.52 us
    pallas_call x1, Pallas kernels: 45.6 us -> 36.4 us  [per_device(): pl.pallas_call(functools.partial(kernel, seq_count, width // heads), out_...]
    unnamed x11 -> x10, local copies, waits for them, and re-layouts: 4.34 us -> 3.52 us
    broadcast_in_dim x1 -> x0, local copies, waits for them, and re-layouts: 0.67 us -> none  [per_device(): jnp.broadcast_to(rate_log[:, None], (heads, 128))]
    slice x1 -> x0, local copies, waits for them, and re-layouts: 0.62 us -> none  [per_device(): return (gx[None], gp[None], gs[:, None], gr[:, 0])]
where the time goes in v3:
time: 40.8 us; the launch traced here: 40.6 us
  Pallas kernels  36.4 us (89%)
  local copies, waits for them, and re-layouts  3.52 us (9%)
  between operations  0.65 us (2%)
    pallas_call x1, Pallas kernels, per_device(): pl.pallas_call(functools.partial(kernel, seq_count, width // heads), out_...  36.4 us
    unnamed x10, local copies, waits for them, and re-layouts  3.52 us

profile of v3, /device:TPU:0, one launch (start us, length us, event | category | flops | bytes accessed | tf_op | source)
XLA Modules:
  0.0 40.6 jit_solution(9377272689245389772)
XLA Ops:
  0.6 36.4 %shard_map.84 = (bf16[128,1024]{1,0:T(8,128)(2,1)}, bf16[128,256]{1,0:T(8,128)(2,1)}, f32[16,128]{1,0:T(8,128)}, f32[1,16]{1,0:T(1,128)}) custom-call(bf16[128,1024]{1,0:T(8,128)(2,1)} %bitcast.11, bf16[128,256]{1,0:T(8,128)(2,1)} %bitcast.15, f32[16,128]{1,0:T(8,128)} %bitcast.16, f32[1,16]{1,0:T(1,128)} %bitcast.18, bf16[128,1024]{1,0:T(8,128)(2,1)} %bitcast.12), custom_call_target="tpu_custom_call" | custom-call | tf_op jit(solution)/shard_map/pallas_call | solution.py:373
  37.0 0.0 copy-start
  37.1 1.7 %copy.14 = bf16[1,128,1024]{2,1,0:T(8,128)(2,1)} copy(bf16[1,128,1024]{2,1,0:T(8,128)(2,1)} %bitcast.13) | data formatting | bytes 524288
  38.8 0.0 copy-done
  38.8 0.0 copy-start.1
  38.8 0.6 %copy.15 = bf16[1,128,256]{2,1,0:T(8,128)(2,1)} copy(bf16[1,128,256]{2,1,0:T(8,128)(2,1)S(1)} %bitcast.14) | data formatting | bytes 131072
  39.4 0.1 copy-done.1
  39.5 0.0 copy-start.2
  39.5 0.6 %copy.16 = f32[16,1,128]{2,1,0:T(1,128)} copy(f32[16,1,128]{2,1,0:T(1,128)S(1)} %bitcast.17) | data formatting | bytes 16384
  40.1 0.0 copy-done.2
  40.1 0.5 %copy.17 = f32[16]{0:T(128)} copy(f32[16]{0:T(128)S(1)} %bitcast.19) | data formatting | bytes 128
Async XLA Ops:
  37.0 1.7 %copy-start = (bf16[128,256]{1,0:T(8,128)(2,1)S(1)}, bf16[128,256]{1,0:T(8,128)(2,1)}, u32[]{:S(2)}) copy-start(bf16[128,256]{1,0:T(8,128)(2,1)} %get-tuple-element.9) | copy-start | bytes 196612
  38.8 0.7 %copy-start.1 = (f32[16,128]{1,0:T(8,128)S(1)}, f32[16,128]{1,0:T(8,128)}, u32[]{:S(2)}) copy-start(f32[16,128]{1,0:T(8,128)} %get-tuple-element.10) | copy-start | bytes 24580
  39.5 0.6 %copy-start.2 = (f32[1,16]{1,0:T(1,128)S(1)}, f32[1,16]{1,0:T(1,128)}, u32[]{:S(2)}) copy-start(f32[1,16]{1,0:T(1,128)} %get-tuple-element.11) | copy-start | bytes 196

commit v4 on v3

--- a/solution.py
+++ b/solution.py
@@ -161,6 +161,7 @@
         for p in range(first_pair, end_pair):
             lanes = slice(p * 128, (p + 1) * 128)
             xs, gs = x_ref[:, lanes], g_ref[:, lanes]
+            twice = jnp.concatenate([gs, gs], axis=0)
             grown = jnp.zeros((span, 128), F32)
             for part in range(per):
                 h = p * per + part
@@ -173,7 +174,7 @@
                 total_scores = total_scores + flow * fade
                 from_rows.append(jnp.sum(flow * weight, axis=0, keepdims=True))
                 high, low = split(weight)
-                grown = jnp.where(mine, dot(high, gs) + dot(low, gs), grown)
+                grown = jnp.where(mine, dot(jnp.concatenate([high, low], axis=1), twice), grown)
             du_ref[:, lanes] = grown
         return total_scores
 
@@ -181,14 +182,20 @@
     for copy in news:
         copy.wait()
     few = heads // 2
-    wide_step, wide_cum, decays = [], [], []
+    wide_step = []
     rate_half = jnp.where(core == 0, rate[:few], rate[few:])
     for r in range(4):
         step_r = softplus(jnp.where(core == 0, raws[r, :few], raws[r, few:]))
         cum_r = lax.dot_general(rate_half * step_r, causal.astype(F32), NN, precision=HIGHEST,
                                 preferred_element_type=F32)
         wide_step.append((step_r, cum_r))
-        decays.append(widen_half(jnp.exp(cum_r))[span - 1:span])
+
+    at_lane = lax.broadcasted_iota(jnp.int32, (few, span), 1)
+    ends = wide_step[3][1][:, span - 1:span]
+    for r in (2, 1, 0):
+        ends = jnp.where(at_lane < (r + 1) * (span // 4), wide_step[r][1][:, span - 1:span], ends)
+    ends = widen_half(jnp.exp(ends))
+    decays = [ends[r * (span // 4):r * (span // 4) + 1] for r in range(4)]
 
     def weigh(r, which):
         step_r, cum_r = wide_step[r]
@@ -197,11 +204,14 @@
 
     urgent_weights = [weigh(r, urgent) for r in range(4)]
 
-    def block_state(r, which, k, weight):
+    def block_state(r, which, k, weight, basis):
         lanes = slice(k * CHUNK, (k + 1) * CHUNK)
         high, low = split(quad[r, k, which].astype(F32) * weight[:, lanes])
-        basis = pairs[r, which]
-        parts[r, which, :, lanes] = dot(basis, high, TN) + dot(basis, low, TN)
+        parts[r, which, :, lanes] = dot(basis, jnp.concatenate([high, low], axis=0))
+
+    def turned(r, which):
+        across_span = jnp.transpose(pairs[r, which])
+        return jnp.concatenate([across_span, across_span], axis=1)
 
     def cut(row, k):
         return row[:, k * CHUNK:(k + 1) * CHUNK]
@@ -245,11 +255,12 @@
 
     for copy in basis_first:
         copy.wait()
+    bases = [turned(r, urgent) for r in range(4)]
     for k in range(half):
         for copy in first[k]:
             copy.wait()
         for r in range(4):
-            block_state(r, urgent, k, urgent_weights[r])
+            block_state(r, urgent, k, urgent_weights[r], bases[r])
         if levels == 3:
             put_last(k, whole(urgent, k))
     total_scores = inside(EARLY, width // 128, total_scores)
@@ -260,20 +271,44 @@
     weights = [weigh(r, 1 - urgent) for r in range(4)]
     for copy in basis_second:
         copy.wait()
+    bases = [turned(r, 1 - urgent) for r in range(4)]
     for k in range(half):
         for copy in second[k]:
             copy.wait()
         for r in range(4):
-            block_state(r, 1 - urgent, k, weights[r])
+            block_state(r, 1 - urgent, k, weights[r], bases[r])
     if levels > 3:
         for k in range(half):
             put(2, k, whole(0, k), whole(1, k), all_decay(k))
         outer[...] = jnp.zeros_like(outer)
 
+    last = [None] * chunks
+
+    def finish(q, grad_b, grad_c):
+        lanes = slice(q * CHUNK, (q + 1) * CHUNK)
+        enter, leave = passed[q, 0], passed[q, 1]
+        eh, el = split(enter)
+        lh, ll = split(leave)
+        xs, gs = x_ref[:, lanes].astype(F32), g_ref[:, lanes].astype(F32)
+        step_w, end_w, cum_w = wide[0, :, lanes], wide[1, :, lanes], wide[2, :, lanes]
+        carried = cum_w * (dot(c, eh) + dot(c, el))
+        later = end_w * (dot(b, lh) + dot(b, ll))
+        scaled = xs * step_w
+        oh, ol = split(gs * cum_w)
+        grad_c = grad_c + (dot(oh, eh, NT) + dot(oh, el, NT) + dot(ol, eh, NT))
+        ih, il = split(scaled * end_w)
+        grad_b = grad_b + (dot(ih, lh, NT) + dot(ih, ll, NT) + dot(il, lh, NT))
+        du = du_ref[:, lanes] + later
+        gx_ref[:, lanes] = (du * step_w).astype(BF16)
+        last[q] = (jnp.sum(scaled * later, axis=0, keepdims=True)
+                    + cum_w[span - 1:span] * jnp.sum(enter * leave, axis=0, keepdims=True))
+        wide[2, :, lanes] = gs * carried
+        du_ref[:, lanes] = du * xs
+        return grad_b, grad_c
+
     mate, _ = partner(0)
     ones = jnp.ones((1, CHUNK), F32)
     dp, dq = [ones] * half, [ones] * half
-    moved = []
     for level in range(2, levels):
         up = partner(level)[1] == 1
         for k in range(half):
@@ -308,33 +343,12 @@
             odd = core == 1
             give[k, 0] = jnp.where(odd, enter0, enter1)
             give[k, 1] = jnp.where(odd, leave0, leave1)
-            moved.append(send(give.at[k], passed.at[core * half + k], s_pass, (k,), seq=mate))
+            hand = send(give.at[k], passed.at[core * half + k], s_pass, (k,), seq=mate)
             passed[core * half + k, 0] = jnp.where(odd, enter1, enter0)
             passed[core * half + k, 1] = jnp.where(odd, leave1, leave0)
-    for copy in moved:
-        copy.wait()
-
-    last = []
-    for q in range(chunks):
-        lanes = slice(q * CHUNK, (q + 1) * CHUNK)
-        enter, leave = passed[q, 0], passed[q, 1]
-        eh, el = split(enter)
-        lh, ll = split(leave)
-        xs, gs = x_ref[:, lanes].astype(F32), g_ref[:, lanes].astype(F32)
-        step_w, end_w, cum_w = wide[0, :, lanes], wide[1, :, lanes], wide[2, :, lanes]
-        carried = cum_w * (dot(c, eh) + dot(c, el))
-        later = end_w * (dot(b, lh) + dot(b, ll))
-        scaled = xs * step_w
-        oh, ol = split(gs * cum_w)
-        grad_c = grad_c + (dot(oh, eh, NT) + dot(oh, el, NT) + dot(ol, eh, NT))
-        ih, il = split(scaled * end_w)
-        grad_b = grad_b + (dot(ih, lh, NT) + dot(ih, ll, NT) + dot(il, lh, NT))
-        du = du_ref[:, lanes] + later
-        gx_ref[:, lanes] = (du * step_w).astype(BF16)
-        last.append(jnp.sum(scaled * later, axis=0, keepdims=True)
-                    + cum_w[span - 1:span] * jnp.sum(enter * leave, axis=0, keepdims=True))
-        wide[2, :, lanes] = gs * carried
-        du_ref[:, lanes] = du * xs
+            hand.wait()
+            for q in (k, half + k):
+                grad_b, grad_c = finish(q, grad_b, grad_c)
     mine = jnp.where(even, grad_b, grad_c)
     pair_s[...] = jnp.where(even, grad_c, grad_b)
     trade = send(pair_s, pair_r, s_pair, (), tensor=buddy)

time: 40.8 us -> 41.1 us (level)
  no operation moved by 1% of the time
where the time goes in v4:
time: 41.1 us; the launch traced here: 40.9 us
  Pallas kernels  36.8 us (90%)
  local copies, waits for them, and re-layouts  3.52 us (9%)
  between operations  0.65 us (2%)
    pallas_call x1, Pallas kernels, per_device(): pl.pallas_call(functools.partial(kernel, seq_count, width // heads), out_...  36.8 us
    unnamed x10, local copies, waits for them, and re-layouts  3.52 us

profile of v4, /device:TPU:0, one launch (start us, length us, event | category | flops | bytes accessed | tf_op | source)
XLA Modules:
  0.0 40.9 jit_solution(10020978861504387958)
XLA Ops:
  0.6 36.8 %shard_map.84 = (bf16[128,1024]{1,0:T(8,128)(2,1)}, bf16[128,256]{1,0:T(8,128)(2,1)}, f32[16,128]{1,0:T(8,128)}, f32[1,16]{1,0:T(1,128)}) custom-call(bf16[128,1024]{1,0:T(8,128)(2,1)} %bitcast.11, bf16[128,256]{1,0:T(8,128)(2,1)} %bitcast.15, f32[16,128]{1,0:T(8,128)} %bitcast.16, f32[1,16]{1,0:T(1,128)} %bitcast.18, bf16[128,1024]{1,0:T(8,128)(2,1)} %bitcast.12), custom_call_target="tpu_custom_call" | custom-call | tf_op jit(solution)/shard_map/pallas_call | solution.py:387
  37.4 0.0 copy-start
  37.4 1.7 %copy.14 = bf16[1,128,1024]{2,1,0:T(8,128)(2,1)} copy(bf16[1,128,1024]{2,1,0:T(8,128)(2,1)} %bitcast.13) | data formatting | bytes 524288
  39.1 0.0 copy-done
  39.1 0.0 copy-start.1
  39.1 0.6 %copy.15 = bf16[1,128,256]{2,1,0:T(8,128)(2,1)} copy(bf16[1,128,256]{2,1,0:T(8,128)(2,1)S(1)} %bitcast.14) | data formatting | bytes 131072
  39.7 0.1 copy-done.1
  39.8 0.0 copy-start.2
  39.8 0.6 %copy.16 = f32[16,1,128]{2,1,0:T(1,128)} copy(f32[16,1,128]{2,1,0:T(1,128)S(1)} %bitcast.17) | data formatting | bytes 16384
  40.4 0.0 copy-done.2
  40.4 0.5 %copy.17 = f32[16]{0:T(128)} copy(f32[16]{0:T(128)S(1)} %bitcast.19) | data formatting | bytes 128
Async XLA Ops:
  37.4 1.7 %copy-start = (bf16[128,256]{1,0:T(8,128)(2,1)S(1)}, bf16[128,256]{1,0:T(8,128)(2,1)}, u32[]{:S(2)}) copy-start(bf16[128,256]{1,0:T(8,128)(2,1)} %get-tuple-element.9) | copy-start | bytes 196612
  39.1 0.7 %copy-start.1 = (f32[16,128]{1,0:T(8,128)S(1)}, f32[16,128]{1,0:T(8,128)}, u32[]{:S(2)}) copy-start(f32[16,128]{1,0:T(8,128)} %get-tuple-element.10) | copy-start | bytes 24580
  39.8 0.6 %copy-start.2 = (f32[1,16]{1,0:T(1,128)S(1)}, f32[1,16]{1,0:T(1,128)}, u32[]{:S(2)}) copy-start(f32[1,16]{1,0:T(1,128)} %get-tuple-element.11) | copy-start | bytes 196

commit v5 on v4

--- a/solution.py
+++ b/solution.py
@@ -92,7 +92,13 @@
 
     def share_basis(which, at):
         return [send(pairs.at[place, which], pairs.at[place, which], s_proj, (at, i), seq=to)
-                for i, to, _ in peers]
+                for i, to, _ in peers if i != 2]
+
+    def forward_basis(copies, which, at):
+        copies[0].wait()
+        facing = place + 2 - 4 * across
+        return [send(pairs.at[facing, which], pairs.at[facing, which], s_proj, (at, 2), seq=peers[2][1]),
+                copies[1]]
 
     first, second = [share(0, urgent, s_first)], []
     quad[place] = stage[core]
@@ -253,7 +259,7 @@
             sent[level, k] = send(tots.at[level - 2, k], totr.at[level - 2, k], s_tot,
                                   (level - 2, k), seq=partner(level)[0])
 
-    for copy in basis_first:
+    for copy in forward_basis(basis_first, urgent, 0):
         copy.wait()
     bases = [turned(r, urgent) for r in range(4)]
     for k in range(half):
@@ -263,6 +269,7 @@
             block_state(r, urgent, k, urgent_weights[r], bases[r])
         if levels == 3:
             put_last(k, whole(urgent, k))
+    basis_second = forward_basis(basis_second, 1 - urgent, 1)
     total_scores = inside(EARLY, width // 128, total_scores)
     row_part = jnp.concatenate(from_rows, axis=0)
     high, low = split(total_scores)

time: 41.1 us -> 41.2 us (level)
  no operation moved by 1% of the time
where the time goes in v5:
time: 41.2 us; the launch traced here: 40.9 us
  Pallas kernels  36.8 us (89%)
  local copies, waits for them, and re-layouts  3.52 us (9%)
  between operations  0.65 us (2%)
    pallas_call x1, Pallas kernels, per_device(): pl.pallas_call(functools.partial(kernel, seq_count, width // heads), out_...  36.8 us
    unnamed x10, local copies, waits for them, and re-layouts  3.52 us

profile of v5, /device:TPU:0, one launch (start us, length us, event | category | flops | bytes accessed | tf_op | source)
XLA Modules:
  0.0 40.9 jit_solution(10305234320494213635)
XLA Ops:
  0.6 36.8 %shard_map.84 = (bf16[128,1024]{1,0:T(8,128)(2,1)}, bf16[128,256]{1,0:T(8,128)(2,1)}, f32[16,128]{1,0:T(8,128)}, f32[1,16]{1,0:T(1,128)}) custom-call(bf16[128,1024]{1,0:T(8,128)(2,1)} %bitcast.11, bf16[128,256]{1,0:T(8,128)(2,1)} %bitcast.15, f32[16,128]{1,0:T(8,128)} %bitcast.16, f32[1,16]{1,0:T(1,128)} %bitcast.18, bf16[128,1024]{1,0:T(8,128)(2,1)} %bitcast.12), custom_call_target="tpu_custom_call" | custom-call | tf_op jit(solution)/shard_map/pallas_call | solution.py:394
  37.4 0.0 copy-start
  37.4 1.7 %copy.14 = bf16[1,128,1024]{2,1,0:T(8,128)(2,1)} copy(bf16[1,128,1024]{2,1,0:T(8,128)(2,1)} %bitcast.13) | data formatting | bytes 524288
  39.1 0.0 copy-done
  39.1 0.0 copy-start.1
  39.1 0.6 %copy.15 = bf16[1,128,256]{2,1,0:T(8,128)(2,1)} copy(bf16[1,128,256]{2,1,0:T(8,128)(2,1)S(1)} %bitcast.14) | data formatting | bytes 131072
  39.8 0.1 copy-done.1
  39.8 0.0 copy-start.2
  39.8 0.6 %copy.16 = f32[16,1,128]{2,1,0:T(1,128)} copy(f32[16,1,128]{2,1,0:T(1,128)S(1)} %bitcast.17) | data formatting | bytes 16384
  40.4 0.0 copy-done.2
  40.4 0.5 %copy.17 = f32[16]{0:T(128)} copy(f32[16]{0:T(128)S(1)} %bitcast.19) | data formatting | bytes 128
Async XLA Ops:
  37.4 1.7 %copy-start = (bf16[128,256]{1,0:T(8,128)(2,1)S(1)}, bf16[128,256]{1,0:T(8,128)(2,1)}, u32[]{:S(2)}) copy-start(bf16[128,256]{1,0:T(8,128)(2,1)} %get-tuple-element.9) | copy-start | bytes 196612
  39.1 0.7 %copy-start.1 = (f32[16,128]{1,0:T(8,128)S(1)}, f32[16,128]{1,0:T(8,128)}, u32[]{:S(2)}) copy-start(f32[16,128]{1,0:T(8,128)} %get-tuple-element.10) | copy-start | bytes 24580
  39.8 0.6 %copy-start.2 = (f32[1,16]{1,0:T(1,128)S(1)}, f32[1,16]{1,0:T(1,128)}, u32[]{:S(2)}) copy-start(f32[1,16]{1,0:T(1,128)} %get-tuple-element.11) | copy-start | bytes 196
